TPU v7x, 32 devices: a whole 2x2x4 slice. The times are simulated.
32 devices in a mesh: ctx: 2 (over x), fsdp: 16 (over z, y, core).
Axes of the slice: x: 2, y: 2, z: 4, core: 2. Of those that a mesh axis runs over, the one named last changes fastest.
Arguments:
- tokens_in: bfloat16 [2, 16, 512, 768], P(None, None, ('ctx', 'fsdp')), may hold values from -6 to 6
- out_grad: bfloat16 [2, 16, 512, 768], P(None, None, ('ctx', 'fsdp')), may hold values from -6 to 6
- seq_lengths: int32 [2, 16], replicated, may hold values from 257 to 512, as said below
- order: int32 [2, 16], replicated, may hold values from 0 to 15, as said below
- w_qkv: bfloat16 [768, 2304], P('fsdp'), may hold values from -0.21875 to 0.21875
- bias_q: bfloat16 [768], P('fsdp'), may hold values from -3 to 3
- bias_v: bfloat16 [768], P('fsdp'), may hold values from -3 to 3
- w_out: bfloat16 [768, 768], P('fsdp'), may hold values from -0.875 to 0.875
- bias_out: bfloat16 [768], P('fsdp'), may hold values from -3 to 3
- ln1_gain: bfloat16 [768], P('fsdp'), may hold values from 0.5 to 1.5
- ln1_bias: bfloat16 [768], P('fsdp'), may hold values from -2 to 2
- w_gate_up: bfloat16 [768, 6144], P('fsdp'), may hold values from -0.21875 to 0.21875
- w_down: bfloat16 [3072, 768], P('fsdp'), may hold values from -0.21875 to 0.21875
- bias_down: bfloat16 [768], P('fsdp'), may hold values from -3 to 3
- ln2_gain: bfloat16 [768], P('fsdp'), may hold values from 0.5 to 1.5
- ln2_bias: bfloat16 [768], P('fsdp'), may hold values from -2 to 2
Outputs:
- output: bfloat16 [2, 16, 512, 768], P(None, None, ('ctx', 'fsdp'))
- input_grad: bfloat16 [2, 16, 512, 768], P(None, None, ('ctx', 'fsdp'))
- grad_w_qkv: float32 [768, 2304], P('fsdp')
- grad_bias_q: float32 [768], P('fsdp')
- grad_bias_v: float32 [768], P('fsdp')
- grad_w_out: float32 [768, 768], P('fsdp')
- grad_bias_out: float32 [768], P('fsdp')
- grad_ln1_gain: float32 [768], P('fsdp')
- grad_ln1_bias: float32 [768], P('fsdp')
- grad_w_gate_up: float32 [768, 6144], P('fsdp')
- grad_w_down: float32 [3072, 768], P('fsdp')
- grad_bias_down: float32 [768], P('fsdp')
- grad_ln2_gain: float32 [768], P('fsdp')
- grad_ln2_bias: float32 [768], P('fsdp')
Inputs may be any that keep to these rules, and one draw needn't show every extreme that they name: `seq_lengths`: a sequence's real tokens fill its slots 0 to length - 1; in each micro-batch some sequence fills all 512 slots. `order`: each row is a permutation of the micro-batch's sequences.
All inputs are finite; a program needn't handle non-finite values.
Results may differ from a plain program's by a relative error of at most 0.015.
Values may be sent and summed in bfloat16 or wider, within the bound.
A program may use at most 120 MiB of HBM per device.

v0:
```python
import math

import jax
import jax.numpy as jnp
from jax import lax
from jax.sharding import PartitionSpec as P

D = 768
HEADS = 12
HEAD_DIM = 64
FF = 3072
M = 2


EPSILON = 1e-12
NEGATIVE = -1e30


def slope_list(head_count):

    def powers(number):
        anchor = 2.0 ** (-(2.0 ** (-(math.log2(number) - 3))))
        return [anchor ** (power_index + 1) for power_index in range(number)]

    closest = 2 ** int(math.floor(math.log2(head_count)))
    return powers(closest) + powers(2 * closest)[0::2][: head_count - closest]


def layer_norm(inputs, gain_row, offset_row):
    centre = inputs - jnp.mean(inputs, axis=-1, keepdims=True)
    spread = jnp.mean(centre * centre, axis=-1, keepdims=True)
    return centre * lax.rsqrt(spread + EPSILON) * gain_row + offset_row


def gated_unit(gate_up):
    return jax.nn.gelu(gate_up[:, :FF], approximate=False) * gate_up[:, FF:]


def rows_product(former, latter):
    return lax.dot_general(
        former, latter, (((0,), (0,)), ((), ())), preferred_element_type=jnp.float32
    )


def by_transpose(former, latter):
    return lax.dot_general(
        former, latter, (((1,), (1,)), ((), ())), preferred_element_type=jnp.float32
    )


def plain_product(former, latter):
    return jnp.dot(former, latter, preferred_element_type=jnp.float32)


def masked_scores(heads_q, heads_k, position, key_place, length, slopes):
    raw_scores = (
        jnp.einsum("qhd,khd->hqk", heads_q, heads_k, preferred_element_type=jnp.float32) * 0.125
    )
    distance = jnp.abs(position[:, None] - key_place[None, :]).astype(jnp.float32)
    raw_scores = raw_scores - slopes[:, None, None] * distance[None]
    return jnp.where((key_place < length)[None, None, :], raw_scores, NEGATIVE)


def fetch_weights(shards):
    return (
        lax.all_gather(shards[0], "fsdp", axis=0, tiled=True),
        lax.all_gather(shards[1], "fsdp", axis=0, tiled=True),
        lax.all_gather(shards[2], "fsdp", axis=0, tiled=True),
        lax.all_gather(shards[3], "fsdp", axis=0, tiled=True),
        lax.all_gather(shards[4], "fsdp", axis=0, tiled=True),
        lax.all_gather(shards[5], "fsdp", axis=0, tiled=True),
        lax.all_gather(shards[6], "fsdp", axis=0, tiled=True),
        lax.all_gather(shards[7], "fsdp", axis=0, tiled=True),
        lax.all_gather(shards[8], "fsdp", axis=0, tiled=True),
        lax.all_gather(shards[9], "fsdp", axis=0, tiled=True),
        lax.all_gather(shards[10], "fsdp", axis=0, tiled=True),
        lax.all_gather(shards[11], "fsdp", axis=0, tiled=True),
    )


def reduce_grads(grad_terms):
    shard_sums = (
        lax.psum_scatter(grad_terms[0], "fsdp", scatter_dimension=0, tiled=True),
        lax.psum_scatter(grad_terms[1], "fsdp", scatter_dimension=0, tiled=True),
        lax.psum_scatter(grad_terms[2], "fsdp", scatter_dimension=0, tiled=True),
        lax.psum_scatter(grad_terms[3], "fsdp", scatter_dimension=0, tiled=True),
        lax.psum_scatter(grad_terms[4], "fsdp", scatter_dimension=0, tiled=True),
        lax.psum_scatter(grad_terms[5], "fsdp", scatter_dimension=0, tiled=True),
        lax.psum_scatter(grad_terms[6], "fsdp", scatter_dimension=0, tiled=True),
        lax.psum_scatter(grad_terms[7], "fsdp", scatter_dimension=0, tiled=True),
        lax.psum_scatter(grad_terms[8], "fsdp", scatter_dimension=0, tiled=True),
        lax.psum_scatter(grad_terms[9], "fsdp", scatter_dimension=0, tiled=True),
        lax.psum_scatter(grad_terms[10], "fsdp", scatter_dimension=0, tiled=True),
        lax.psum_scatter(grad_terms[11], "fsdp", scatter_dimension=0, tiled=True),
    )
    return (
        lax.psum(shard_sums[0].astype(jnp.bfloat16), "ctx").astype(jnp.float32),
        lax.psum(shard_sums[1].astype(jnp.bfloat16), "ctx").astype(jnp.float32),
        lax.psum(shard_sums[2].astype(jnp.bfloat16), "ctx").astype(jnp.float32),
        lax.psum(shard_sums[3].astype(jnp.bfloat16), "ctx").astype(jnp.float32),
        lax.psum(shard_sums[4].astype(jnp.bfloat16), "ctx").astype(jnp.float32),
        lax.psum(shard_sums[5].astype(jnp.bfloat16), "ctx").astype(jnp.float32),
        lax.psum(shard_sums[6].astype(jnp.bfloat16), "ctx").astype(jnp.float32),
        lax.psum(shard_sums[7].astype(jnp.bfloat16), "ctx").astype(jnp.float32),
        lax.psum(shard_sums[8].astype(jnp.bfloat16), "ctx").astype(jnp.float32),
        lax.psum(shard_sums[9].astype(jnp.bfloat16), "ctx").astype(jnp.float32),
        lax.psum(shard_sums[10].astype(jnp.bfloat16), "ctx").astype(jnp.float32),
        lax.psum(shard_sums[11].astype(jnp.bfloat16), "ctx").astype(jnp.float32),
    )


def per_device(
    tokens_in,
    out_grad,
    seq_lengths,
    order,
    w_qkv,
    bias_q,
    bias_v,
    w_out,
    bias_out,
    ln1_gain,
    ln1_bias,
    w_gate_up,
    w_down,
    bias_down,
    ln2_gain,
    ln2_bias,
):
    shards = (
        w_qkv,
        bias_q,
        bias_v,
        w_out,
        bias_out,
        ln1_gain,
        ln1_bias,
        w_gate_up,
        w_down,
        bias_down,
        ln2_gain,
        ln2_bias,
    )
    group_index = lax.axis_index("fsdp")
    ctx_index = lax.axis_index("ctx")
    dealt_tokens = jnp.take_along_axis(tokens_in, order[:, :, None, None], axis=1)
    tokens_grp, grads_grp = (
        lax.all_to_all(dealt_tokens, "fsdp", split_axis=1, concat_axis=2, tiled=True),
        lax.all_to_all(out_grad, "fsdp", split_axis=1, concat_axis=2, tiled=True),
    )
    dealt_lengths = jnp.take_along_axis(seq_lengths, order, axis=1)
    local_rows = tokens_grp.shape[2]
    key_place = jnp.arange(local_rows * lax.axis_size("ctx"))
    position = ctx_index * local_rows + jnp.arange(local_rows)
    slopes = jnp.array(slope_list(HEADS), jnp.float32)
    output_list = []
    input_list = []
    running = None
    for micro_batch in range(M):
        weights = fetch_weights(shards)
        (
            full_qkv,
            full_bias_q,
            full_bias_v,
            full_out,
            full_bias_out,
            full_ln1_gain,
            full_ln1_bias,
            full_gate_up,
            full_down,
            full_bias_down,
            full_ln2_gain,
            full_ln2_bias,
        ) = weights
        tokens = tokens_grp[micro_batch, 0]
        cotangent = grads_grp[micro_batch, 0]
        length = lax.dynamic_index_in_dim(
            dealt_lengths[micro_batch], group_index, 0, keepdims=False
        )
        valid_rows = position < length
        projected = plain_product(tokens, full_qkv)
        queries = (projected[:, :D] + full_bias_q.astype(jnp.float32)).astype(jnp.bfloat16)
        key_rows = projected[:, D : 2 * D].astype(jnp.bfloat16)
        values = (projected[:, 2 * D :] + full_bias_v.astype(jnp.float32)).astype(jnp.bfloat16)
        keys_all, values_all = (
            lax.all_gather(key_rows, "ctx", axis=0, tiled=True),
            lax.all_gather(values, "ctx", axis=0, tiled=True),
        )
        heads_q = queries.reshape(local_rows, HEADS, HEAD_DIM)
        heads_k = keys_all.reshape(-1, HEADS, HEAD_DIM)
        heads_v = values_all.reshape(-1, HEADS, HEAD_DIM)
        scores = masked_scores(heads_q, heads_k, position, key_place, length, slopes)
        row_max = jnp.max(scores, axis=-1, keepdims=True)
        exp_terms = jnp.exp(scores - row_max)
        row_total = jnp.sum(exp_terms, axis=-1, keepdims=True)
        log_total = row_max + jnp.log(row_total)
        attn_probs = (exp_terms / row_total).astype(jnp.bfloat16)
        context = (
            jnp.einsum("hqk,khd->qhd", attn_probs, heads_v, preferred_element_type=jnp.float32)
            .reshape(local_rows, D)
            .astype(jnp.bfloat16)
        )
        attn_out = plain_product(context, full_out) + full_bias_out.astype(jnp.float32)
        first_sum = tokens.astype(jnp.float32) + attn_out
        normed_one, norm_one_pull = jax.vjp(
            layer_norm,
            first_sum,
            full_ln1_gain.astype(jnp.float32),
            full_ln1_bias.astype(jnp.float32),
        )
        normed_low = normed_one.astype(jnp.bfloat16)
        gate_up = plain_product(normed_low, full_gate_up)
        hidden, gated_pull = jax.vjp(gated_unit, gate_up)
        hidden_low = hidden.astype(jnp.bfloat16)
        branch = plain_product(hidden_low, full_down) + full_bias_down.astype(jnp.float32)
        result, norm_two_pull = jax.vjp(
            layer_norm,
            normed_one + branch,
            full_ln2_gain.astype(jnp.float32),
            full_ln2_bias.astype(jnp.float32),
        )
        output_list.append(jnp.where(valid_rows[:, None], result, 0.0).astype(jnp.bfloat16))
        grad_result = jnp.where(valid_rows[:, None], cotangent.astype(jnp.float32), 0.0)
        grad_second, grad_ln2_gain, grad_ln2_bias = norm_two_pull(grad_result)
        grad_branch = grad_second.astype(jnp.bfloat16)
        grad_bias_down = jnp.sum(grad_branch.astype(jnp.float32), axis=0)
        grad_w_down = rows_product(hidden_low, grad_branch)
        grad_hidden = by_transpose(grad_branch, full_down)
        (grad_gate_up,) = gated_pull(grad_hidden)
        grad_gate_low = grad_gate_up.astype(jnp.bfloat16)
        grad_w_gate_up = rows_product(normed_low, grad_gate_low)
        grad_normed = grad_second + by_transpose(grad_gate_low, full_gate_up)
        grad_first, grad_ln1_gain, grad_ln1_bias = norm_one_pull(grad_normed)
        grad_attn = grad_first.astype(jnp.bfloat16)
        grad_bias_out = jnp.sum(grad_attn.astype(jnp.float32), axis=0)
        grad_w_out = rows_product(context, grad_attn)
        grad_context = (
            by_transpose(grad_attn, full_out)
            .astype(jnp.bfloat16)
            .reshape(local_rows, HEADS, HEAD_DIM)
        )
        scores = masked_scores(heads_q, heads_k, position, key_place, length, slopes)
        attn_exact = jnp.exp(scores - log_total)
        grad_values_term = jnp.einsum(
            "hqk,qhd->khd",
            attn_exact.astype(jnp.bfloat16),
            grad_context,
            preferred_element_type=jnp.float32,
        )
        grad_probs = jnp.einsum(
            "qhd,khd->hqk", grad_context, heads_v, preferred_element_type=jnp.float32
        )
        grad_scores = (
            attn_exact * (grad_probs - jnp.sum(attn_exact * grad_probs, axis=-1, keepdims=True))
        ).astype(jnp.bfloat16)
        grad_queries = (
            jnp.einsum("hqk,khd->qhd", grad_scores, heads_k, preferred_element_type=jnp.float32)
            * 0.125
        ).reshape(local_rows, D)
        grad_keys_term = (
            jnp.einsum("hqk,qhd->khd", grad_scores, heads_q, preferred_element_type=jnp.float32)
            * 0.125
        )
        grad_keys, grad_values = (
            lax.psum_scatter(
                grad_keys_term.reshape(-1, D).astype(jnp.bfloat16),
                "ctx",
                scatter_dimension=0,
                tiled=True,
            ).astype(jnp.float32),
            lax.psum_scatter(
                grad_values_term.reshape(-1, D).astype(jnp.bfloat16),
                "ctx",
                scatter_dimension=0,
                tiled=True,
            ).astype(jnp.float32),
        )
        grad_qkv = jnp.concatenate(
            [
                grad_queries.astype(jnp.bfloat16),
                grad_keys.astype(jnp.bfloat16),
                grad_values.astype(jnp.bfloat16),
            ],
            axis=1,
        )
        grad_w_qkv = rows_product(tokens, grad_qkv)
        grad_bias_q = jnp.sum(grad_qkv[:, :D].astype(jnp.float32), axis=0)
        grad_bias_v = jnp.sum(grad_qkv[:, 2 * D :].astype(jnp.float32), axis=0)
        grad_tokens = grad_first + by_transpose(grad_qkv, full_qkv)
        input_list.append(grad_tokens.astype(jnp.bfloat16))
        grad_terms = (
            grad_w_qkv,
            grad_bias_q,
            grad_bias_v,
            grad_w_out,
            grad_bias_out,
            grad_ln1_gain,
            grad_ln1_bias,
            grad_w_gate_up,
            grad_w_down,
            grad_bias_down,
            grad_ln2_gain,
            grad_ln2_bias,
        )
        reduced = reduce_grads(grad_terms)
        if micro_batch == 0:
            running = reduced
        else:
            running = tuple((left_sum + right_sum for left_sum, right_sum in zip(running, reduced)))
    output_stack = jnp.stack(output_list, axis=0)[:, None]
    input_stack = jnp.stack(input_list, axis=0)[:, None]
    output, dealt_grads = (
        lax.all_to_all(output_stack, "fsdp", split_axis=2, concat_axis=1, tiled=True),
        lax.all_to_all(input_stack, "fsdp", split_axis=2, concat_axis=1, tiled=True),
    )
    inverse = jnp.argsort(order, axis=1)
    input_grad = jnp.take_along_axis(dealt_grads, inverse[:, :, None, None], axis=1)
    return (
        output,
        input_grad,
        running[0],
        running[1],
        running[2],
        running[3],
        running[4],
        running[5],
        running[6],
        running[7],
        running[8],
        running[9],
        running[10],
        running[11],
    )


def solution(mesh):
    return jax.shard_map(
        per_device,
        mesh=mesh,
        in_specs=(
            P(None, None, ("ctx", "fsdp"), None),
            P(None, None, ("ctx", "fsdp"), None),
            P(),
            P(),
            P("fsdp", None),
            P("fsdp"),
            P("fsdp"),
            P("fsdp", None),
            P("fsdp"),
            P("fsdp"),
            P("fsdp"),
            P("fsdp", None),
            P("fsdp", None),
            P("fsdp"),
            P("fsdp"),
            P("fsdp"),
        ),
        out_specs=(
            P(None, None, ("ctx", "fsdp"), None),
            P(None, None, ("ctx", "fsdp"), None),
            P("fsdp", None),
            P("fsdp"),
            P("fsdp"),
            P("fsdp", None),
            P("fsdp"),
            P("fsdp"),
            P("fsdp"),
            P("fsdp", None),
            P("fsdp", None),
            P("fsdp"),
            P("fsdp"),
            P("fsdp"),
        ),
        check_vma=False,
    )
```

profile of v0, /device:TPU:0, one launch (start us, length us, event | category | flops | bytes accessed | tf_op | source)
XLA Modules:
  0.0 1450.4 jit_solution(6775887001916883405)
XLA Ops:
  12.8 7.4 all-to-all-start
  24.0 72.8 %all-reduce.29 = (bf16[768]{0:T(1024)(128)(2,1)S(1)}, bf16[768]{0:T(1024)(128)(2,1)S(1)}, bf16[768]{0:T(1024)(128)(2,1)S(1)}, bf16[768]{0:T(1024)(128)(2,1)S(1)}...) all-reduce(bf16[768]{0:T(1024)(128)(2,1)S(1)} %dynamic-update-slice, ...), channel_id=1, replica_groups=mesh['ctx'=2,'fsdp'=16] {'fsdp'}, use_global_device_ids=true, to_apply=%add.4 | all-reduce | flops 6144 | bytes 24576
  105.7 3.6 all-to-all-start.2
  109.5 3.2 fusion.100
  114.2 12.0 all_gather.75
  126.4 3.4 fusion.99
  133.6 11.5 all_gather.64
  146.3 10.8 all_gather.74
  158.2 9.7 all_gather.62
  169.2 3.0 fusion.96
  174.8 2.8 fusion.43
  177.7 2.1 fusion.97
  184.3 2.2 fusion.42
  188.0 11.6 all-gather.9.cloned.1.call-done
  199.6 5.5 fusion.79
  206.1 2.7 fusion.82
  208.8 7.9 multiply_convert_fusion.2
  216.7 8.4 multiply_convert_fusion.3
  225.0 28.2 %all-gather.11.cloned.1.call-done = bf16[3072,768]{1,0:T(8,128)(2,1)} async-done(((bf16[192,768]{1,0:T(8,128)(2,1)}), bf16[3072,768]{1,0:T(8,128)(2,1)}) %all-gather.11.cloned.1.call-update) | async-done | bytes 4718608 | tf_op jit(solution)/shard_map/all_gather | solution.py:74
  253.3 4.5 fusion.95
  260.5 2.9 multiply_reduce_fusion.2
  263.4 3.3 fusion.87
  269.1 9.1 fusion.47
  278.2 6.7 fusion.46
  285.0 6.9 convolution_add_fusion.6
  291.9 7.9 multiply_reduce_fusion.5
  301.2 2.8 fusion.84
  307.7 1.9 copy.84
  309.6 5.0 fusion.28
  314.6 5.2 multiply_reduce_fusion.1
  319.9 3.8 multiply_convert_fusion.1
  327.0 1.9 convert_reduce_fusion.2
  332.1 4.9 fusion.31
  337.1 4.1 multiply_reduce_fusion
  341.2 3.7 multiply_convert_fusion
  350.2 3.0 fusion.101
  353.2 4.3 convert_reduce_fusion.7
  357.6 5.3 fusion.57
  364.0 3.7 convert_reduce_fusion.6
  367.7 3.6 reduce-scatter.19.cloned.1.call-done
  371.3 20.4 %reduce-scatter.17.cloned.1.call-done = bf16[256,768]{0,1:T(8,128)(2,1)} async-done(((bf16[512,768]{0,1:T(8,128)(2,1)}), bf16[256,768]{0,1:T(8,128)(2,1)}) %reduce-scatter.17.cloned.1.call-update) | async-done | bytes 393232 | tf_op jit(solution)/shard_map/reduce_scatter | solution.py:265
  391.6 5.1 fusion.56
  397.7 6.5 fusion.104
  405.2 6.4 fusion.103
  411.7 12.4 fusion.59
  424.2 12.1 fusion.58
  439.2 5.7 all-to-all-start.1
  455.3 12.5 all-to-all-done.1
  468.8 4.0 fusion.44
  475.6 56.1 %reduce-scatter.25.cloned.1.call-done = f32[48,768]{1,0:T(8,128)} async-done(((f32[768,768]{1,0:T(8,128)}), f32[48,768]{1,0:T(8,128)}) %reduce-scatter.25.cloned.1.call-update) | async-done | bytes 147472 | tf_op jit(solution)/shard_map/reduce_scatter | solution.py:86
  533.3 91.6 %reduce-scatter.21.cloned.1.call-done = f32[48,2304]{1,0:T(8,128)} async-done(((f32[768,2304]{1,0:T(8,128)}), f32[48,2304]{1,0:T(8,128)}) %reduce-scatter.21.cloned.1.call-update) | async-done | bytes 442384 | tf_op jit(solution)/shard_map/reduce_scatter | solution.py:83
  626.6 92.3 %reduce-scatter.23.cloned.1.call-done = f32[48,2304]{1,0:T(8,128)} async-done(((f32[768,2304]{1,0:T(8,128)}), f32[48,2304]{1,0:T(8,128)}) %reduce-scatter.23.cloned.1.call-update) | async-done | bytes 442384 | tf_op jit(solution)/shard_map/reduce_scatter | solution.py:83
  720.6 113.3 %reduce-scatter.35.cloned.1.call-done = f32[192,768]{1,0:T(8,128)} async-done(((f32[3072,768]{1,0:T(8,128)}), f32[192,768]{1,0:T(8,128)}) %reduce-scatter.35.cloned.1.call-update) | async-done | bytes 589840 | tf_op jit(solution)/shard_map/reduce_scatter | solution.py:91
  835.7 113.8 %reduce-scatter.33.cloned.1.call-done = f32[192,768]{1,0:T(8,128)} async-done(((f32[3072,768]{1,0:T(8,128)}), f32[192,768]{1,0:T(8,128)}) %reduce-scatter.33.cloned.1.call-update) | async-done | bytes 589840 | tf_op jit(solution)/shard_map/reduce_scatter | solution.py:91
  951.4 196.9 %reduce-scatter.31.cloned.1.call-done = f32[48,6144]{1,0:T(8,128)} async-done(((f32[768,6144]{1,0:T(8,128)}), f32[48,6144]{1,0:T(8,128)}) %reduce-scatter.31.cloned.1.call-update) | async-done | bytes 1179664 | tf_op jit(solution)/shard_map/reduce_scatter | solution.py:90
  1148.2 2.1 convert_element_type.506
  1150.4 195.9 %reduce-scatter.29.cloned.1.call-done = f32[48,6144]{1,0:T(8,128)} async-done(((f32[768,6144]{1,0:T(8,128)}), f32[48,6144]{1,0:T(8,128)}) %reduce-scatter.29.cloned.1.call-update) | async-done | bytes 1179664 | tf_op jit(solution)/shard_map/reduce_scatter | solution.py:90
  1346.2 2.1 convert_element_type.504
  1350.8 59.9 %all-reduce.28 = (bf16[768]{0:T(1024)(128)(2,1)S(1)}, bf16[768]{0:T(1024)(128)(2,1)S(1)}, bf16[768]{0:T(1024)(128)(2,1)S(1)}, bf16[768]{0:T(1024)(128)(2,1)S(1)}...) all-reduce(f32[768]{0:T(1024)S(1)} %copy-done.73, ...), channel_id=9, replica_groups=mesh['ctx'=2,'fsdp'=16] {'fsdp'}, use_global_device_ids=true, to_apply=%region_35.37.clone | all-reduce | flops 12288 | bytes 73728
  1411.9 3.6 all-to-all-start.3
  1415.5 5.1 all-reduce.30
  1424.7 9.5 all-to-all-done.3
  1439.4 1.9 convert_add_fusion.1
  1441.3 2.4 convert_add_fusion
  (405 shorter events, 99.0 us)
Async XLA Ops:
  7.2 102.3 %all-gather.5.cloned.1.call-start = ((), (), s32[]{:S(2)}) async-start(), calls=%async_computation.16 | async-start | bytes 3760128 | tf_op jit(solution)/shard_map/all_gather | solution.py:66
  7.9 169.7 %all-gather.7.cloned.1.call-start = ((), (), s32[]{:S(2)}) async-start(), calls=%async_computation.17 | async-start | bytes 1253376 | tf_op jit(solution)/shard_map/all_gather | solution.py:69
  8.7 190.9 %all-gather.9.cloned.1.call-start = ((), (), s32[]{:S(2)}) async-start(), calls=%async_computation.18 | async-start | bytes 10027008 | tf_op jit(solution)/shard_map/all_gather | solution.py:73
  10.2 10.6 copy-start.92
  10.2 11.9 copy-start.95
  10.2 12.1 copy-start.96
  10.2 12.3 copy-start.97
  10.2 12.6 copy-start.98
  10.2 12.8 copy-start.99
  10.2 13.0 copy-start.100
  10.2 13.2 copy-start.101
  10.3 13.5 copy-start.102
  10.3 86.6 %copy-start.2 = (s32[2,16]{1,0:T(2,128)S(1)}, s32[2,16]{1,0:T(2,128)}, u32[]{:S(2)}) copy-start(s32[2,16]{1,0:T(2,128)} %param.21) | copy-start | bytes 388
  10.9 86.8 %copy-start.80 = (s32[2,16]{1,0:T(2,128)S(1)}, s32[2,16]{1,0:T(2,128)}, u32[]{:S(2)}) copy-start(s32[2,16]{1,0:T(2,128)} %param.22) | copy-start | bytes 388
  10.9 89.7 %copy-start.55 = (bf16[2,16,16,768]{3,2,1,0:T(8,128)(2,1)S(1)}, bf16[2,16,16,768]{3,2,1,0:T(8,128)(2,1)}, u32[]{:S(2)}) copy-start(bf16[2,16,16,768]{3,2,1,0:T(8,128)(2,1)} %param.20) | copy-start | bytes 2359300
  12.8 92.9 %all-to-all-start = ((bf16[2,16,16,768]{3,2,0,1:T(8,128)(2,1)}), bf16[2,16,16,768]{3,2,0,1:T(8,128)(2,1)S(1)}, u32[]{:S(2)}, u32[]{:S(2)}) async-start(bf16[2,16,16,768]{3,2,0,1:T(8,128)(2,1)} %copy.73), calls=%async_computation | async-start | bytes 1572864 | tf_op jit(solution)/shard_map/all_to_all | solution.py:148
  20.2 233.0 %all-gather.11.cloned.1.call-start = ((), (), s32[]{:S(2)}) async-start(), calls=%async_computation.19 | async-start | bytes 5013504 | tf_op jit(solution)/shard_map/all_gather | solution.py:74
  105.7 154.7 %all-to-all-start.2 = ((bf16[2,16,16,768]{3,2,0,1:T(8,128)(2,1)}), bf16[2,16,16,768]{3,2,0,1:T(8,128)(2,1)S(1)}, u32[]{:S(2)}, u32[]{:S(2)}) async-start(bf16[2,16,16,768]{3,2,0,1:T(8,128)(2,1)} %copy.83), calls=%async_computation.2 | async-start | bytes 1572864 | tf_op jit(solution)/shard_map/all_to_all | solution.py:149
  109.4 248.2 %reduce-scatter.15.cloned.1.call-start = ((), (), s32[]{:S(2)}) async-start(), calls=%async_computation.21 | async-start | bytes 1179648 | tf_op jit(solution)/shard_map/reduce_scatter | solution.py:271
  109.5 68.2 %copy-start.20 = (bf16[1,16,16,768]{3,2,0,1:T(8,128)(2,1)}, bf16[1,16,16,768]{3,2,0,1:T(8,128)(2,1)S(1)}, u32[]{:S(2)}) copy-start(bf16[1,16,16,768]{3,2,0,1:T(8,128)(2,1)S(1)} %get-tuple-element.140) | copy-start | bytes 1179652
  126.4 53.5 %copy-start.29 = (bf16[512,768]{0,1:T(8,128)(2,1)}, bf16[512,768]{0,1:T(8,128)(2,1)S(1)}, u32[]{:S(2)}) copy-start(bf16[512,768]{0,1:T(8,128)(2,1)S(1)} %copy.79) | copy-start | bytes 2359300
  146.3 22.9 %copy-start.103 = (f32[12]{0:T(128)S(1)}, f32[12]{0:T(128)}, u32[]{:S(2)}) copy-start(f32[12]{0:T(128)} %constant.142.clone) | copy-start | bytes 148
  179.9 7.5 copy-start.76
  188.0 65.2 %copy-start.62 = (f32[256]{0:T(256)}, f32[256]{0:T(256)S(1)}, u32[]{:S(2)}) copy-start(f32[256]{0:T(256)S(1)} %fusion.68) | copy-start | bytes 3076
  208.8 7.9 copy-start.9
  216.7 36.6 %copy-start.88 = (f32[768]{0:T(1024)S(1)}, f32[768]{0:T(1024)}, u32[]{:S(2)}) copy-start(f32[768]{0:T(1024)} %convert_element_type.420) | copy-start | bytes 9220
  266.7 11.5 copy-start.35
  267.6 10.6 copy-start.40
  267.6 10.6 slice-start.3
  269.1 9.1 slice-start.4
  269.1 9.1 copy-start.27
  269.1 15.9 %slice-start = ((s8[9437184]{0:T(1024)(128)(4,1)}), s8[4194304]{0:T(1024)(128)(4,1)S(1)}, s32[]{:S(2)}) async-start(s8[9437184]{0:T(1024)(128)(4,1)} %bitcast.160), calls=%async_computation.33 | async-start | bytes 8388608
  269.1 15.8 %slice-start.1 = ((s8[9437184]{0:T(1024)(128)(4,1)}), s8[4194304]{0:T(1024)(128)(4,1)S(1)}, s32[]{:S(2)}) async-start(s8[9437184]{0:T(1024)(128)(4,1)} %bitcast.160), calls=%async_computation.34 | async-start | bytes 8388608
  284.9 6.9 copy-start.26
  285.0 6.9 copy-start.63
  291.9 7.9 copy-start.79
  291.9 8.7 copy-start.77
  304.0 10.6 copy-start.89
  314.6 43.0 %reduce-scatter.13.cloned.1.call-start = ((), (), s32[]{:S(2)}) async-start(), calls=%async_computation.20 | async-start | bytes 1179648 | tf_op jit(solution)/shard_map/reduce_scatter | solution.py:265
  327.0 44.3 %reduce-scatter.19.cloned.1.call-start = ((), (), s32[]{:S(2)}) async-start(), calls=%async_computation.23 | async-start | bytes 1179648 | tf_op jit(solution)/shard_map/reduce_scatter | solution.py:271
  327.0 9.9 copy-start.91
  337.0 54.6 %reduce-scatter.17.cloned.1.call-start = ((), (), s32[]{:S(2)}) async-start(), calls=%async_computation.22 | async-start | bytes 1179648 | tf_op jit(solution)/shard_map/reduce_scatter | solution.py:265
  348.1 125.9 %reduce-scatter.27.cloned.1.call-start = ((), (), s32[]{:S(2)}) async-start(), calls=%async_computation.27 | async-start | bytes 2506752 | tf_op jit(solution)/shard_map/reduce_scatter | solution.py:86
  350.1 181.6 %reduce-scatter.25.cloned.1.call-start = ((), (), s32[]{:S(2)}) async-start(), calls=%async_computation.26 | async-start | bytes 2506752 | tf_op jit(solution)/shard_map/reduce_scatter | solution.py:86
  353.2 271.7 %reduce-scatter.21.cloned.1.call-start = ((), (), s32[]{:S(2)}) async-start(), calls=%async_computation.24 | async-start | bytes 7520256 | tf_op jit(solution)/shard_map/reduce_scatter | solution.py:83
  362.9 356.0 %reduce-scatter.23.cloned.1.call-start = ((), (), s32[]{:S(2)}) async-start(), calls=%async_computation.25 | async-start | bytes 7520256 | tf_op jit(solution)/shard_map/reduce_scatter | solution.py:83
  367.7 29.0 %copy-start.44 = (bf16[12,64,256]{2,1,0:T(8,128)(2,1)}, bf16[12,64,256]{2,1,0:T(8,128)(2,1)S(1)}, u32[]{:S(2)}) copy-start(bf16[12,64,256]{2,1,0:T(8,128)(2,1)S(1)} %get-tuple-element.173) | copy-start | bytes 1179652
  396.7 437.2 %reduce-scatter.35.cloned.1.call-start = ((), (), s32[]{:S(2)}) async-start(), calls=%async_computation.31 | async-start | bytes 10027008 | tf_op jit(solution)/shard_map/reduce_scatter | solution.py:91
  404.2 545.3 %reduce-scatter.33.cloned.1.call-start = ((), (), s32[]{:S(2)}) async-start(), calls=%async_computation.30 | async-start | bytes 10027008 | tf_op jit(solution)/shard_map/reduce_scatter | solution.py:91
  411.7 736.6 %reduce-scatter.31.cloned.1.call-start = ((), (), s32[]{:S(2)}) async-start(), calls=%async_computation.29 | async-start | bytes 20054016 | tf_op jit(solution)/shard_map/reduce_scatter | solution.py:90
  424.1 922.1 %reduce-scatter.29.cloned.1.call-start = ((), (), s32[]{:S(2)}) async-start(), calls=%async_computation.28 | async-start | bytes 20054016 | tf_op jit(solution)/shard_map/reduce_scatter | solution.py:90
  436.3 8.8 copy-start.81
  436.3 16.1 %copy-start.14 = (bf16[2,16,16,768]{3,2,0,1:T(8,128)(2,1)S(1)}, bf16[2,16,16,768]{3,2,0,1:T(8,128)(2,1)}, u32[]{:S(2)}) copy-start(bf16[2,16,16,768]{3,2,0,1:T(8,128)(2,1)} %copy-done.13) | copy-start | bytes 2359300
  436.4 18.3 %copy-start.65 = (f32[12,64]{1,0:T(8,128)S(1)}, f32[12,64]{1,0:T(8,128)}, u32[]{:S(2)}) copy-start(f32[12,64]{1,0:T(8,128)} %get-tuple-element.174) | copy-start | bytes 9220
  437.5 31.2 %copy-start.34 = (f32[256,768]{1,0:T(8,128)S(1)}, f32[256,768]{1,0:T(8,128)}, u32[]{:S(2)}) copy-start(f32[256,768]{1,0:T(8,128)} %get-tuple-element.145) | copy-start | bytes 2359300
  437.5 31.2 %copy-start.45 = (bf16[12,64,256]{2,1,0:T(8,128)(2,1)S(1)}, bf16[12,64,256]{2,1,0:T(8,128)(2,1)}, u32[]{:S(2)}) copy-start(bf16[12,64,256]{2,1,0:T(8,128)(2,1)} %copy-done.44) | copy-start | bytes 1179652
  437.5 31.2 %copy-start.47 = (bf16[256,768]{0,1:T(8,128)(2,1)S(1)}, bf16[256,768]{0,1:T(8,128)(2,1)}, u32[]{:S(2)}) copy-start(bf16[256,768]{0,1:T(8,128)(2,1)} %reduce-scatter.19.cloned.1.call-done) | copy-start | bytes 1179652
  437.5 31.2 %copy-start.58 = (bf16[256,768]{0,1:T(8,128)(2,1)S(1)}, bf16[256,768]{0,1:T(8,128)(2,1)}, u32[]{:S(2)}) copy-start(bf16[256,768]{0,1:T(8,128)(2,1)} %reduce-scatter.17.cloned.1.call-done) | copy-start | bytes 1179652
  439.2 28.6 %all-to-all-start.1 = ((bf16[2,1,256,768]{3,0,1,2:T(2,128)(2,1)}), bf16[2,1,256,768]{3,0,1,2:T(2,128)(2,1)S(1)}, u32[]{:S(2)}, u32[]{:S(2)}) async-start(bf16[2,1,256,768]{3,0,1,2:T(2,128)(2,1)} %copy.80), calls=%async_computation.1 | async-start | bytes 1572864 | tf_op jit(solution)/shard_map/all_to_all | solution.py:313
  444.9 991.0 %all-reduce.34.cloned.1.call-start = ((), (), s32[]{:S(2)}) async-start(), calls=%async_computation.32 | async-start | bytes 4718592 | tf_op jit(solution)/shard_map/psum | solution.py:97
  951.4 397.1 %copy-start.59 = (bf16[1,256,768]{2,1,0:T(8,128)(2,1)S(1)}, bf16[1,256,768]{2,1,0:T(8,128)(2,1)}, u32[]{:S(2)}) copy-start(bf16[1,256,768]{2,1,0:T(8,128)(2,1)} %fusion.44) | copy-start | bytes 1179652
  1350.3 84.6 %copy-start.93 = (pred[2,16]{1,0:T(4,128)(4,1)S(1)}, pred[2,16]{1,0:T(4,128)(4,1)}, u32[]{:S(2)}) copy-start(pred[2,16]{1,0:T(4,128)(4,1)} %and_bitcast_fusion) | copy-start | bytes 100
  1411.9 22.3 %all-to-all-start.3 = ((bf16[2,1,256,768]{3,0,1,2:T(2,128)(2,1)}), bf16[2,1,256,768]{3,0,1,2:T(2,128)(2,1)S(1)}, u32[]{:S(2)}, u32[]{:S(2)}) async-start(bf16[2,1,256,768]{3,0,1,2:T(2,128)(2,1)} %copy.86), calls=%async_computation.7 | async-start | bytes 1572864 | tf_op jit(solution)/shard_map/all_to_all | solution.py:314
  1434.9 8.8 copy-start.1
  (66 other events, 186.8 us)
Sparse Core Ops, SparseCore 0:
  10.3 59.2 all-gather.4
  71.9 37.4 all-gather.6
  111.7 87.9 all-gather.8
  201.8 51.4 all-gather.10
  314.7 15.9 reduce-scatter.14
  333.5 17.4 reduce-scatter.12
  353.8 17.4 reduce-scatter.18
  374.2 17.4 reduce-scatter.16
  395.4 68.1 reduce-scatter.26
  467.7 64.0 reduce-scatter.24
  535.8 89.0 reduce-scatter.20
  629.3 89.5 reduce-scatter.22
  723.0 110.8 reduce-scatter.34
  838.4 111.0 reduce-scatter.32
  953.5 194.6 reduce-scatter.30
  1152.2 193.9 reduce-scatter.28
  1349.9 69.0 all-reduce.33
where the time goes:
time: 1460 us; the launch traced here: 1450 us
  waiting for transfers between devices  948 us (65%)
  blocking collectives  182 us (12%)
  matrix products  154 us (11%)
  other arithmetic  84.6 us (6%)
  local copies, waits for them, and re-layouts  43 us (3%)
  starting transfers between devices  21.5 us (1%)
  between operations  16.9 us (1%)
    reduce_scatter x2, waiting for transfers between devices, reduce_grads(): lax.psum_scatter(grad_terms[7], 'fsdp', scatter_dimension=0, tiled=True)  393 us
    reduce_scatter x2, waiting for transfers between devices, reduce_grads(): lax.psum_scatter(grad_terms[8], 'fsdp', scatter_dimension=0, tiled=True)  227 us
    reduce_scatter x2, waiting for transfers between devices, reduce_grads(): lax.psum_scatter(grad_terms[0], 'fsdp', scatter_dimension=0, tiled=True)  184 us
    unnamed x2, blocking collectives  133 us
    reduce_scatter x2, waiting for transfers between devices, reduce_grads(): lax.psum_scatter(grad_terms[3], 'fsdp', scatter_dimension=0, tiled=True)  56.2 us
    dot_general x8, matrix products, rows_product(): lax.dot_general(former, latter, (((0,), (0,)), ((), ())), preferred_eleme...  52.7 us
    dot_general x8, matrix products, by_transpose(): lax.dot_general(former, latter, (((1,), (1,)), ((), ())), preferred_eleme...  38.2 us
  transfers between devices with their start and end apart: 21, of which 13 were waited for; matrix products, arithmetic and copies ran while one was open for 14% of the time, Pallas kernels for 0%

commit v1 on v0

--- a/solution.py
+++ b/solution.py
@@ -1,8 +1,11 @@
+import functools
 import math
 
 import jax
 import jax.numpy as jnp
 from jax import lax
+from jax.experimental import pallas as pl
+from jax.experimental.pallas import tpu as pltpu
 from jax.sharding import PartitionSpec as P
 
 D = 768
@@ -10,10 +13,13 @@
 HEAD_DIM = 64
 FF = 3072
 M = 2
-
-
 EPSILON = 1e-12
 NEGATIVE = -1e30
+MESH = pl.DeviceIdType.MESH
+BF = jnp.bfloat16
+F32 = jnp.float32
+LOG2E = math.log2(math.e)
+VMEM_LIMIT = 62 << 20
 
 
 def slope_list(head_count):
@@ -109,7 +115,7 @@
     )
 
 
-def per_device(
+def per_device_plain(
     tokens_in,
     out_grad,
     seq_lengths,
@@ -333,9 +339,825 @@
     )
 
 
+W0 = 256
+W1 = 256
+WIN = W0 + W1
+PIECES = 16
+
+
+def mm(a, b):
+    return jnp.dot(a, b, preferred_element_type=F32)
+
+
+def mm_nt(a, b):
+    return lax.dot_general(a, b, (((1,), (1,)), ((), ())), preferred_element_type=F32)
+
+
+def mm_tn(a, b):
+    return lax.dot_general(a, b, (((0,), (0,)), ((), ())), preferred_element_type=F32)
+
+
+def block(i, size):
+    if isinstance(i, int):
+        return pl.ds(i * size, size)
+    return pl.ds(pl.multiple_of(i * size, size), size)
+
+
+class Place:
+    def __init__(self, fsdp):
+        self.fsdp = fsdp
+        self.total = 2 * fsdp
+        self.Z = fsdp // 4
+        self.x = lax.axis_index("ctx")
+        self.f = lax.axis_index("fsdp")
+        self.z = self.f // 4
+        self.y = lax.rem(self.f // 2, 2)
+        self.c = lax.rem(self.f, 2)
+        self.me = self.x * fsdp + self.f
+        self.cols = pl.ds(pl.multiple_of(self.x * W1, 128), WIN)
+        self.give = pl.ds(pl.multiple_of(self.x * WIN, 128), W1)
+        self.take = pl.ds(pl.multiple_of((1 - self.x) * WIN, 128), W1)
+        self.pending = []
+
+    def dev(self, x=None, z=None, y=None, c=None):
+        x = self.x if x is None else x
+        z = self.z if z is None else z
+        y = self.y if y is None else y
+        c = self.c if c is None else c
+        return (x, z * 4 + y * 2 + c)
+
+    def at(self, d):
+        return (d // self.fsdp, lax.rem(d, self.fsdp))
+
+    def barrier(self):
+        sem = pltpu.get_barrier_semaphore()
+
+        @pl.loop(1, self.total)
+        def _(k):
+            d = lax.rem(self.me + k, self.total)
+            pl.semaphore_signal(sem, inc=1, device_id=self.at(d), device_id_type=MESH)
+
+        pl.semaphore_wait(sem, self.total - 1)
+
+    def go(self, copy, cond=None):
+        if cond is None:
+            copy.start()
+        else:
+            pl.when(cond)(copy.start)
+        self.pending.append((cond, copy))
+
+    def finish(self):
+        for cond, copy in self.pending:
+            if cond is None:
+                copy.wait_send()
+            else:
+                pl.when(cond)(copy.wait_send)
+        self.pending = []
+
+
+def remote(src, dst, send, recv, device):
+    return pltpu.make_async_remote_copy(
+        src_ref=src, dst_ref=dst, send_sem=send, recv_sem=recv, device_id=device, device_id_type=MESH
+    )
+
+
+class Exchange:
+    def __init__(self, pc, src, dst, sems, k, one=False):
+        self.pc, self.src, self.dst, self.one = pc, src, dst, one
+        self.send, self.recv, self.local = sems[0].at[k], sems[1].at[k], sems[2].at[k]
+
+    def part(self, d):
+        return self.src if self.one else self.src.at[d]
+
+    def own(self):
+        return pltpu.make_async_copy(self.part(self.pc.me), self.dst.at[self.pc.me], self.local)
+
+    def start(self):
+        pc = self.pc
+        self.own().start()
+
+        @pl.loop(1, pc.total)
+        def _(k):
+            d = lax.rem(pc.me + k, pc.total)
+            remote(self.part(d), self.dst.at[pc.me], self.send, self.recv, pc.at(d)).start()
+
+    def whole(self):
+        r = self.dst.at[pl.ds(0, self.pc.total - 1)]
+        return remote(r, r, self.send, self.recv, self.pc.dev(c=1 - self.pc.c))
+
+    def wait(self):
+        self.own().wait()
+        self.whole().wait_recv()
+
+    def done(self):
+        self.whole().wait_send()
+
+
+class Gather:
+    def __init__(self, pc, own, slots, sems):
+        self.pc, self.own, self.slots = pc, own, slots
+        self.zs, self.zr, self.ys, self.yr, self.xs, self.xr, self.cs, self.cr, self.ls = sems
+
+    @staticmethod
+    def sems(Z):
+        T = pltpu.SemaphoreType.DMA
+        n = PIECES
+        return [
+            T((n, 2 * Z - 2)), T((n, 2 * Z - 2)), T((n, 2 * Z - 1)), T((n,)),
+            T((n,)), T((n,)), T((n, 2)), T((n, 2)), T((n,)),
+        ]
+
+    def up(self):
+        return jnp.minimum(self.pc.z + 1, self.pc.Z - 1)
+
+    def down(self):
+        return jnp.maximum(self.pc.z - 1, 0)
+
+    def mine(self, p):
+        pc = self.pc
+        src = self.own(p, pc.cols)
+        dst = self.slots(p, pc.z, pc.y, pc.c, pc.cols)
+        return pltpu.make_async_copy(src, dst, self.ls.at[p])
+
+    def start(self, p):
+        pc = self.pc
+        Z = pc.Z
+        src = self.own(p, pc.cols)
+        dst = self.slots(p, pc.z, pc.y, pc.c, pc.cols)
+        self.mine(p).start()
+        pc.go(remote(src, dst, self.zs.at[p, 0], self.zr.at[p, 0], pc.dev(z=self.up())), pc.z < Z - 1)
+        k = Z - 1
+        pc.go(remote(src, dst, self.zs.at[p, k], self.zr.at[p, k], pc.dev(z=self.down())), pc.z > 0)
+        pc.go(remote(src, dst, self.ys.at[p, 0], self.yr.at[p], pc.dev(y=1 - pc.y)))
+
+    def hop(self, p, h):
+        pc = self.pc
+        Z = pc.Z
+        for upward in (True, False):
+            k = (0 if upward else Z - 1) + h - 1
+            if upward:
+                z, here, onward, to = jnp.maximum(pc.z - h, 0), pc.z >= h, pc.z < Z - 1, self.up()
+            else:
+                z, here, onward, to = jnp.minimum(pc.z + h, Z - 1), pc.z + h < Z, pc.z > 0, self.down()
+            ref = self.slots(p, z, pc.y, pc.c, pc.cols)
+            pl.when(here)(remote(ref, ref, self.zs.at[p, k], self.zr.at[p, k], pc.dev(z=to)).wait_recv)
+            if h < Z - 1:
+                pc.go(
+                    remote(ref, ref, self.zs.at[p, k + 1], self.zr.at[p, k + 1], pc.dev(z=to)),
+                    jnp.logical_and(here, onward),
+                )
+            pc.go(remote(ref, ref, self.ys.at[p, 1 + k], self.yr.at[p], pc.dev(y=1 - pc.y)), here)
+
+    def row(self, p):
+        pc = self.pc
+        ref = self.slots(p, slice(None), 1 - pc.y, pc.c, pc.cols)
+        remote(ref, ref, self.ys.at[p, 0], self.yr.at[p], pc.dev(y=1 - pc.y)).wait_recv()
+        self.mine(p).wait()
+        ref = self.slots(p, slice(None), slice(None), pc.c, pc.give)
+        pc.go(remote(ref, ref, self.xs.at[p], self.xr.at[p], pc.dev(x=1 - pc.x)))
+        ref = self.slots(p, slice(None), slice(None), pc.c, pc.cols)
+        pc.go(remote(ref, ref, self.cs.at[p, 0], self.cr.at[p, 0], pc.dev(c=1 - pc.c)))
+
+    def plane(self, p):
+        pc = self.pc
+        ref = self.slots(p, slice(None), slice(None), pc.c, pc.take)
+        remote(ref, ref, self.xs.at[p], self.xr.at[p], pc.dev(x=1 - pc.x)).wait_recv()
+        pc.go(remote(ref, ref, self.cs.at[p, 1], self.cr.at[p, 1], pc.dev(c=1 - pc.c)))
+
+    def core(self, p):
+        pc = self.pc
+        for k, cols in ((0, pc.cols), (1, pc.take)):
+            ref = self.slots(p, slice(None), slice(None), 1 - pc.c, cols)
+            remote(ref, ref, self.cs.at[p, k], self.cr.at[p, k], pc.dev(c=1 - pc.c)).wait_recv()
+
+
+class Scatter:
+    def __init__(self, pc, acc, from_c, from_x, from_y, from_z, from_f, sems):
+        self.pc, self.acc = pc, acc
+        self.from_c, self.from_x, self.from_y, self.from_z, self.from_f = from_c, from_x, from_y, from_z, from_f
+        self.cs, self.cr, self.xs, self.xr, self.ys, self.yr, self.zs, self.zr, self.fs, self.fr, self.ls = sems
+        z = pc.z
+        self.inner = jnp.logical_or(z == 1, z == 2)
+        self.outer = jnp.logical_not(self.inner)
+        self.mate = z + 1 - 2 * lax.rem(z, 2)
+        self.far_in = jnp.where(z < 2, 2, 1)
+        self.far_out = jnp.where(z < 2, 3, 0)
+
+    @staticmethod
+    def sems():
+        T = pltpu.SemaphoreType.DMA
+        n = PIECES
+        return [
+            T((n,)), T((n,)), T((n,)), T((n,)), T((n,)), T((n,)), T((n, 5)), T((n, 4)), T((n,)), T((n,)), T((n,)),
+        ]
+
+    @staticmethod
+    def buffers(Z, rows):
+        n = PIECES
+        return [
+            pltpu.VMEM((n, Z, 2, rows, D), BF),
+            pltpu.VMEM((n, Z, 2, rows, D), BF),
+            pltpu.VMEM((n, Z, 2, rows, W1), BF),
+            pltpu.VMEM((n, Z, rows, WIN), BF),
+            pltpu.VMEM((n, 4, rows, WIN), BF),
+            pltpu.VMEM((n, rows, WIN), BF),
+        ]
+
+    def load(self, p, terms):
+        return pltpu.make_async_copy(terms(self.pc.c), self.acc.at[p], self.ls.at[p])
+
+    def start(self, p, terms):
+        pc = self.pc
+        pc.go(remote(terms(1 - pc.c), self.from_c.at[p], self.cs.at[p], self.cr.at[p], pc.dev(c=1 - pc.c)))
+
+    def core(self, p):
+        pc = self.pc
+        ref = self.from_c.at[p]
+        remote(ref, ref, self.cs.at[p], self.cr.at[p], pc.dev(c=1 - pc.c)).wait_recv()
+
+        @pl.loop(0, 2 * pc.Z)
+        def _(k):
+            z, y = k // 2, lax.rem(k, 2)
+            self.acc[p, z, y] = self.acc[p, z, y] + self.from_c[p, z, y]
+
+        src = self.acc.at[p, :, :, :, pc.take]
+        pc.go(remote(src, self.from_x.at[p], self.xs.at[p], self.xr.at[p], pc.dev(x=1 - pc.x)))
+
+    def plane(self, p):
+        pc = self.pc
+        ref = self.from_x.at[p]
+        remote(ref, ref, self.xs.at[p], self.xr.at[p], pc.dev(x=1 - pc.x)).wait_recv()
+
+        @pl.loop(0, 2 * pc.Z)
+        def _(k):
+            z, y = k // 2, lax.rem(k, 2)
+            self.acc[p, z, y, :, pc.give] = self.acc[p, z, y, :, pc.give] + self.from_x[p, z, y]
+
+        src = self.acc.at[p, :, 1 - pc.y, :, pc.cols]
+        pc.go(remote(src, self.from_y.at[p], self.ys.at[p], self.yr.at[p], pc.dev(y=1 - pc.y)))
+
+    def row(self, p):
+        pc = self.pc
+        ref = self.from_y.at[p]
+        remote(ref, ref, self.ys.at[p], self.yr.at[p], pc.dev(y=1 - pc.y)).wait_recv()
+
+        @pl.loop(0, pc.Z)
+        def _(z):
+            self.acc[p, z, pc.y, :, pc.cols] = self.acc[p, z, pc.y, :, pc.cols] + self.from_y[p, z]
+
+        for k, z in enumerate((self.mate, self.far_in, self.far_out)):
+            src = self.acc.at[p, z, pc.y, :, pc.cols]
+            pc.go(
+                remote(src, self.from_z.at[p, k], self.zs.at[p, k], self.zr.at[p, k], pc.dev(z=self.mate)),
+                self.outer if k else None,
+            )
+
+    def middle(self, p):
+        pc = self.pc
+        far = ((1, self.far_in), (2, self.far_out))
+
+        @pl.when(self.inner)
+        def _():
+            for k, z in far:
+                ref = self.from_z.at[p, k]
+                remote(ref, ref, self.zs.at[p, k], self.zr.at[p, k], pc.dev(z=self.mate)).wait_recv()
+                self.acc[p, z, pc.y, :, pc.cols] = self.acc[p, z, pc.y, :, pc.cols] + self.from_z[p, k]
+
+        for k, z in far:
+            src = self.acc.at[p, z, pc.y, :, pc.cols]
+            pc.go(
+                remote(src, self.from_z.at[p, 3], self.zs.at[p, 2 + k], self.zr.at[p, 3], pc.dev(z=z)), self.inner
+            )
+
+    def line(self, p):
+        pc = self.pc
+        for k in (0, 3):
+            ref = self.from_z.at[p, k]
+            remote(ref, ref, self.zs.at[p, k], self.zr.at[p, k], pc.dev(z=self.mate)).wait_recv()
+            self.acc[p, pc.z, pc.y, :, pc.cols] = self.acc[p, pc.z, pc.y, :, pc.cols] + self.from_z[p, k]
+        src = self.acc.at[p, pc.z, pc.y, :, pc.cols]
+        pc.go(remote(src, self.from_f.at[p], self.fs.at[p], self.fr.at[p], pc.dev(x=1 - pc.x)))
+
+    def last(self, p, out):
+        pc = self.pc
+        ref = self.from_f.at[p]
+        remote(ref, ref, self.fs.at[p], self.fr.at[p], pc.dev(x=1 - pc.x)).wait_recv()
+        own = self.acc.at[p, pc.z, pc.y]
+        out[:, pc.give] = own[:, pc.give].astype(F32)
+        theirs = pl.ds(pl.multiple_of((1 - pc.x) * W0, 128), W1)
+        out[:, pc.take] = self.from_f[p, :, theirs].astype(F32)
+        both = pl.ds(pl.multiple_of(pc.x * W1, 128), W0)
+        shared = pl.ds(W1, W0)
+        out[:, shared] = own[:, shared].astype(F32) + self.from_f[p, :, both].astype(F32)
+
+
+def row_mean(v):
+    return jnp.sum(v, axis=-1, keepdims=True) * (1.0 / D)
+
+
+BQ, BV, BO, G1, B1, BD, G2, B2 = range(8)
+
+
+def forward_kernel(
+    fsdp, rows,
+    length, slopes, tokens_in, grads_in, small_in, wq_in, wo_in, wg_in, wd_in,
+    X, QKV, DO, LSE, H1G, OUT, WQKV, DWA, DWD, SMALLG,
+    wa, wd, xs, gs, small, smallf, qkv, dist, lse, ctxt, y1, y1b, xhat, rstd, act, slope_up, zed, acc,
+    dfb, tr, *sems,
+):
+    pc = Place(fsdp)
+    Z = pc.Z
+    L = pc.total * tokens_in.shape[1]
+    gsems, esems, osem = sems[:9], sems[9:12], sems[12]
+    w_pc = wa.shape[1:]
+
+    def own(p, cols):
+        if p < 3:
+            return wq_in.at[:, pl.ds(pl.multiple_of(D * p + cols.start, 128), cols.size)]
+        if p == 3:
+            return wo_in.at[:, cols]
+        if p < 12:
+            i, j = (p - 4) // 2, (p - 4) % 2
+            return wg_in.at[:, pl.ds(pl.multiple_of(FF * j + D * i + cols.start, 128), cols.size)]
+        return wd_in.at[pl.ds(rows * (p - 12), rows), cols]
+
+    def slots(p, z, y, c, cols):
+        if p < 12:
+            return wa.at[p, z, y, c, :, cols]
+        return wd.at[z, y, c, p - 12, :, cols]
+
+    def w_cols(p, cols):
+        return wa[p, :, :, :, :, cols].reshape(D, cols.size)
+
+    def w_all(p):
+        return wa[p].reshape(D, D)
+
+    g = Gather(pc, own, slots, gsems)
+    ex_x = Exchange(pc, tokens_in, xs, esems, 0)
+    ex_g = Exchange(pc, grads_in, gs, esems, 1)
+    len_s = length[0]
+
+    def tokens(r):
+        n = r.size // 16
+        return xs[pl.ds(r.start // 16, n)].reshape(r.size, D)
+
+    def prepare():
+        k = lax.broadcasted_iota(jnp.int32, (L, L), 0)
+        q = lax.broadcasted_iota(jnp.int32, (L, L), 1)
+        dist[...] = jnp.where(k < len_s, jnp.abs(k - q).astype(F32), -NEGATIVE)
+
+    def sum_small():
+        def add(i, v):
+            return v + small[i].astype(F32)
+
+        smallf[...] = lax.fori_loop(1, fsdp, add, small[0].astype(F32))
+
+    def project(p):
+        @pl.loop(0, D // 256)
+        def _(t):
+            cols = block(t, 256)
+            r = mm(xs[...].reshape(L, D), w_cols(p, cols))
+            if p != 1:
+                r = r + smallf[pl.ds(BQ if p == 0 else BV, 1), cols]
+            qkv[p, :, cols] = r.astype(BF)
+
+    def attend(j):
+        cols = block(j, 128)
+        lane = lax.broadcasted_iota(jnp.int32, (L, 128), 1)
+        q2, k2 = qkv[0, :, cols], qkv[1, :, cols]
+        vt = qkv[2, :, cols].T
+        for q in range(L // 256):
+            qr = pl.ds(256 * q, 256)
+            parts = []
+            for s in range(2):
+                qm = jnp.where((lane < 64) if s == 0 else (lane >= 64), q2, jnp.zeros_like(q2))
+                st = mm_nt(k2, qm[256 * q : 256 * q + 256])
+                st = st * (0.125 * LOG2E) - dist[:, qr] * slopes[2 * j + s]
+                top = jnp.max(st, axis=0, keepdims=True)
+                e = jnp.exp2(st - top)
+                total = jnp.sum(e, axis=0, keepdims=True)
+                lse[2 * j + s, :, qr] = top + jnp.log2(total)
+                pr = (e * (1.0 / total)).astype(BF)
+                parts.append(mm(vt[64 * s : 64 * s + 64], pr))
+            ctxt[qr, cols] = jnp.concatenate(parts, axis=0).T.astype(BF)
+
+    def first_norm():
+        @pl.loop(0, D // 256)
+        def _(t):
+            cols = block(t, 256)
+            acc[:, cols] = mm(ctxt[...], w_cols(3, cols)) + smallf[pl.ds(BO, 1), cols]
+
+        @pl.loop(0, L // 64)
+        def _(i):
+            r = block(i, 64)
+            h = acc[r, :] + tokens(r).astype(F32)
+            centre = h - row_mean(h)
+            rs = lax.rsqrt(row_mean(centre * centre) + EPSILON)
+            xh = centre * rs
+            xhat[r, :] = xh
+            rstd[r, :] = jnp.broadcast_to(rs, (64, 128))
+            yy = xh * smallf[pl.ds(G1, 1), :] + smallf[pl.ds(B1, 1), :]
+            y1[r, :] = yy
+            y1b[r, :] = yy.astype(BF)
+
+    def gated(i, s):
+        wc = block(s, 256)
+        cols = block(i * 3 + s, 256)
+        a = mm(y1b[...], w_cols(4 + 2 * i, wc))
+        u = mm(y1b[...], w_cols(5 + 2 * i, wc))
+        cdf = 0.5 + 0.5 * lax.erf(a * math.sqrt(0.5))
+        pdf = jnp.exp2(a * a * (-0.5 * LOG2E)) * (1.0 / math.sqrt(2.0 * math.pi))
+        gelu = a * cdf
+        zed[:, cols] = (gelu * u).astype(BF)
+        act[:, cols] = gelu.astype(BF)
+        slope_up[:, cols] = (u * (cdf + a * pdf)).astype(BF)
+
+    def second_norm():
+        @pl.loop(0, D // 256)
+        def _(t):
+            cols = block(t, 256)
+            w = wd[:, :, :, :, :, cols].reshape(FF, 256)
+            acc[:, cols] = mm(zed[...], w) + smallf[pl.ds(BD, 1), cols]
+
+        def step(i, sums):
+            r = block(i, 64)
+            h = acc[r, :] + y1[r, :]
+            centre = h - row_mean(h)
+            rs = lax.rsqrt(row_mean(centre * centre) + EPSILON)
+            xh = centre * rs
+            gain = smallf[pl.ds(G2, 1), :]
+            valid = (lax.broadcasted_iota(jnp.int32, (64, D), 0) + i * 64) < len_s
+            res = jnp.where(valid, xh * gain + smallf[pl.ds(B2, 1), :], 0.0).astype(BF)
+            OUTV[pl.ds(i * 4, 4)] = res.reshape(4, 16, D)
+            up = jnp.where(valid, gs[pl.ds(i * 4, 4)].reshape(64, D).astype(F32), 0.0)
+            dx = up * gain
+            dh = rs * (dx - row_mean(dx) - xh * row_mean(dx * xh))
+            low = dh.astype(BF)
+            acc[r, :] = dh
+            dfb[r, :] = low
+            sg, sb, sd = sums
+            return (
+                sg + jnp.sum(up * xh, axis=0, keepdims=True),
+                sb + jnp.sum(up, axis=0, keepdims=True),
+                sd + jnp.sum(low.astype(F32), axis=0, keepdims=True),
+            )
+
+        zero = jnp.zeros((1, D), F32)
+        sg, sb, sd = lax.fori_loop(0, L // 64, step, (zero, zero, zero))
+        sgrad[pl.ds(G2, 1), :] = sg
+        sgrad[pl.ds(B2, 1), :] = sb
+        sgrad[pl.ds(BD, 1), :] = sd
+
+    def ff_back():
+        tr[...] = y1b[...].T
+
+        @pl.loop(0, FF // D)
+        def _(i):
+            cols = block(i, D)
+            down = wd.at[pl.ds(i * Z // 4, Z // 4)]
+            dz = mm_nt(dfb[...], down[...].reshape(D, D))
+            dgate = (dz * slope_up[:, cols].astype(F32)).astype(BF)
+            dup = (dz * act[:, cols].astype(F32)).astype(BF)
+            acc[...] += mm_nt(dgate, w_all(4 + 2 * i)) + mm_nt(dup, w_all(5 + 2 * i))
+            down[...] = mm_tn(zed[:, cols], dfb[...]).astype(BF).reshape(down.shape)
+            wa[4 + 2 * i] = mm(tr[...], dgate).astype(BF).reshape(w_pc)
+            wa[5 + 2 * i] = mm(tr[...], dup).astype(BF).reshape(w_pc)
+
+    def first_norm_back():
+        def step(i, sums):
+            r = block(i, 64)
+            up = acc[r, :]
+            xh = xhat[r, :]
+            dx = up * smallf[pl.ds(G1, 1), :]
+            dh = rstd[r, :][:, :1] * (dx - row_mean(dx) - xh * row_mean(dx * xh))
+            low = dh.astype(BF)
+            xhat[r, :] = dh
+            dfb[r, :] = low
+            sg, sb, sd = sums
+            return (
+                sg + jnp.sum(up * xh, axis=0, keepdims=True),
+                sb + jnp.sum(up, axis=0, keepdims=True),
+                sd + jnp.sum(low.astype(F32), axis=0, keepdims=True),
+            )
+
+        zero = jnp.zeros((1, D), F32)
+        sg, sb, sd = lax.fori_loop(0, L // 64, step, (zero, zero, zero))
+        sgrad[pl.ds(G1, 1), :] = sg
+        sgrad[pl.ds(B1, 1), :] = sb
+        sgrad[pl.ds(BO, 1), :] = sd
+
+    def out_back():
+        @pl.loop(0, 1)
+        def _(t):
+            y1b[...] = mm_nt(dfb[...], w_all(3)).astype(BF)
+            wa[3] = mm_tn(ctxt[...], dfb[...]).astype(BF).reshape(w_pc)
+
+    OUTV = sems[13]
+    sgrad = sems[14]
+
+    def keep(src, dst, k):
+        c = pltpu.make_async_copy(src, dst, osem.at[k])
+        c.start()
+        kept.append(c)
+
+    kept = []
+
+    pc.barrier()
+    ex_x.start()
+    for k in range(1, fsdp):
+        pass
+
+    me_small = small.at[pc.f]
+    loc = pltpu.make_async_copy(small_in, me_small, esems[2].at[2])
+    loc.start()
+
+    @pl.loop(1, fsdp)
+    def _(k):
+        f = lax.rem(pc.f + k, fsdp)
+        remote(small_in, me_small, esems[0].at[2], esems[1].at[2], (pc.x, f)).start()
+
+    small_all = remote(
+        small.at[pl.ds(0, fsdp - 1)], small.at[pl.ds(0, fsdp - 1)], esems[0].at[2], esems[1].at[2],
+        pc.dev(c=1 - pc.c),
+    )
+
+    def after_core(p):
+        if p == 2:
+            ex_x.wait()
+            small_all.wait_recv()
+            loc.wait()
+            sum_small()
+            prepare()
+            for i in range(3):
+                project(i)
+            keep(xs, X, 0)
+            keep(wa.at[pl.ds(0, 3)], WQKV, 1)
+            keep(qkv, QKV, 2)
+            pl.loop(0, 2)(attend)
+        elif p == 3:
+            pl.loop(2, 5)(attend)
+        elif p == 4:
+            attend(5)
+            first_norm()
+        elif 5 <= p < 12 and p % 2 == 1:
+            for s in range(3):
+                gated((p - 5) // 2, s)
+
+    for t in range(PIECES + 8):
+        if t < PIECES:
+            g.start(t)
+        if t == 4:
+            ex_g.start()
+        for h in range(1, Z):
+            if 0 <= t - h < PIECES:
+                g.hop(t - h, h)
+        if 0 <= t - 4 < PIECES:
+            g.row(t - 4)
+        if 0 <= t - 6 < PIECES:
+            g.plane(t - 6)
+        if 0 <= t - 8 < PIECES:
+            g.core(t - 8)
+            after_core(t - 8)
+    ex_g.wait()
+    pc.finish()
+    second_norm()
+    keep(OUTV, OUT, 3)
+    ff_back()
+    keep(wa.at[pl.ds(4, 8)], DWA.at[pl.ds(1, 8)], 4)
+    keep(wd, DWD, 5)
+    first_norm_back()
+    out_back()
+    keep(wa.at[3], DWA.at[0], 6)
+    keep(y1b, DO, 7)
+    keep(xhat, H1G, 8)
+    keep(lse, LSE, 9)
+    sgrad[pl.ds(BQ, 1), :] = jnp.zeros((1, D), F32)
+    sgrad[pl.ds(BV, 1), :] = jnp.zeros((1, D), F32)
+    keep(sgrad, SMALLG, 10)
+    ex_x.done()
+    ex_g.done()
+    small_all.wait_send()
+    for c in kept:
+        c.wait()
+
+
+def backward_kernel(
+    fsdp, rows,
+    length, slopes, x_in, qkv_in, do_in, lse_in, h1_in, out_in, wqkv_in, dwa, dwd, small_in,
+    GQ, GW, GG, GD, OUT, DX, SMALLG,
+    xs, qkv, dob, lse, h1, wqkv, dist, dqkv, dwq, dxv, sgrad, gsum, *rest,
+):
+    pc = Place(fsdp)
+    bufs, rest = rest[:6], rest[6:]
+    ssems, esems, isem = rest[:11], rest[11:14], rest[14]
+    L = xs.shape[0] * xs.shape[1]
+    sc = Scatter(pc, *bufs, ssems)
+    order = [12, 13, 14, 15] + list(range(4, 12)) + [3, 0, 1, 2]
+
+    def terms(p):
+        if p >= 12:
+            return lambda c: dwd.at[:, :, c, p - 12]
+        if p >= 3:
+            return lambda c: dwa.at[p - 3, :, :, c]
+        return lambda c: dwq.at[p, :, :, c]
+
+    def out_of(p):
+        if p >= 12:
+            return GD.at[pl.ds(rows * (p - 12), rows)]
+        if p == 3:
+            return GW
+        if p < 3:
+            return GQ.at[:, pl.ds(D * p, D)]
+        i, j = (p - 4) // 2, (p - 4) % 2
+        return GG.at[:, pl.ds(FF * j + D * i, D)]
+
+    loads = [
+        pltpu.make_async_copy(s, d, isem.at[k])
+        for k, (s, d) in enumerate(
+            ((x_in, xs), (qkv_in, qkv), (do_in, dob), (lse_in, lse), (h1_in, h1), (wqkv_in, wqkv), (small_in, sgrad))
+        )
+    ]
+    for c in loads:
+        c.start()
+    len_s = length[0]
+    k = lax.broadcasted_iota(jnp.int32, (L, L), 0)
+    q = lax.broadcasted_iota(jnp.int32, (L, L), 1)
+    dist[...] = jnp.where(k < len_s, jnp.abs(k - q).astype(F32), -NEGATIVE)
+
+    def attend_back(j):
+        cols = block(j, 128)
+        lane = lax.broadcasted_iota(jnp.int32, (L, 128), 1)
+        q2, k2, v2 = (qkv[i, :, cols] for i in range(3))
+        do2 = dob[:, cols]
+        kt = k2.T
+        dv = dk = None
+        for q in range(L // 256):
+            qr = pl.ds(256 * q, 256)
+            qs = slice(256 * q, 256 * q + 256)
+            parts = []
+            for s in range(2):
+                half = (lane < 64) if s == 0 else (lane >= 64)
+                qm = jnp.where(half, q2, jnp.zeros_like(q2))[qs]
+                dm = jnp.where(half, do2, jnp.zeros_like(do2))[qs]
+                st = mm_nt(k2, qm) * (0.125 * LOG2E) - dist[:, qr] * slopes[2 * j + s]
+                pr = jnp.exp2(st - lse[2 * j + s, :, qr])
+                dp = mm_nt(v2, dm)
+                ds = (pr * (dp - jnp.sum(pr * dp, axis=0, keepdims=True))).astype(BF)
+                a, b = mm(pr.astype(BF), dm), mm(ds, qm)
+                dv = a if dv is None else dv + a
+                dk = b if dk is None else dk + b
+                parts.append(mm(kt[64 * s : 64 * s + 64], ds))
+            dqkv[0, qr, cols] = (jnp.concatenate(parts, axis=0).T * 0.125).astype(BF)
+        dqkv[1, :, cols] = (dk * 0.125).astype(BF)
+        dqkv[2, :, cols] = dv.astype(BF)
+
+    def weights_back(p):
+        x = xs[...].reshape(L, D)
+        dwq[p] = mm_tn(x, dqkv[p]).astype(BF).reshape(dwq.shape[1:])
+        if p != 1:
+            r = BQ if p == 0 else BV
+            sgrad[pl.ds(r, 1), :] = jnp.sum(dqkv[p].astype(F32), axis=0, keepdims=True)
+
+    def tokens_back():
+        @pl.loop(0, L // 128)
+        def _(i):
+            r = block(i, 128)
+            v = h1[r, :]
+            for p in range(3):
+                v = v + mm_nt(dqkv[p, r, :], wqkv[p].reshape(D, D))
+            dxv[pl.ds(i * 8, 8)] = v.astype(BF).reshape(8, 16, D)
+
+    ex_o = Exchange(pc, out_in, OUT, esems, 0)
+    ex_d = Exchange(pc, dxv, DX, esems, 1)
+    ex_s = Exchange(pc, sgrad, gsum, esems, 2, one=True)
+
+    pc.barrier()
+    for n in range(13):
+        sc.load(order[n], terms(order[n])).start()
+    stages = (("core", 1), ("plane", 3), ("row", 5), ("middle", 6), ("line", 8), ("last", 10))
+    for t in range(PIECES + 10):
+        if t < PIECES:
+            p = order[t]
+            if p < 3:
+                sc.load(p, terms(p)).start()
+            sc.start(p, terms(p))
+        if t == 1:
+            ex_o.start()
+        for name, off in stages:
+            if 0 <= t - off < PIECES:
+                p = order[t - off]
+                if name == "core":
+                    sc.load(p, terms(p)).wait()
+                if name == "last":
+                    sc.last(p, out_of(p))
+                else:
+                    getattr(sc, name)(p)
+        if t == 2:
+            for c in loads:
+                c.wait()
+        if 2 <= t < 8:
+            attend_back(t - 2)
+        if t == 8:
+            tokens_back()
+            ex_d.start()
+        if t == 9:
+            for p in range(3):
+                weights_back(p)
+            ex_s.start()
+    ex_s.wait()
+
+    def add(i, v):
+        return v + gsum[i]
+
+    SMALLG[...] = lax.fori_loop(1, pc.total, add, gsum[0])
+    ex_o.wait()
+    ex_d.wait()
+    for e in (ex_o, ex_d, ex_s):
+        e.done()
+    pc.finish()
+
+
+def per_device(
+    tokens_in, out_grad, seq_lengths, order, w_qkv, bias_q, bias_v, w_out, bias_out, ln1_gain, ln1_bias, w_gate_up,
+    w_down, bias_down, ln2_gain, ln2_bias,
+):
+    fsdp = lax.axis_size("fsdp")
+    total = 2 * fsdp
+    rows = w_out.shape[0]
+    slots_here = tokens_in.shape[2]
+    L = slots_here * total
+    Z = fsdp // 4
+    f = lax.axis_index("fsdp")
+    m = lax.axis_index("ctx")
+    dealt = jnp.take_along_axis(tokens_in, order[:, :, None, None], axis=1).reshape(total, slots_here, D)
+    grads = out_grad.reshape(total, slots_here, D)
+    length = seq_lengths[m, order[m, f]].reshape(1)
+    slopes = jnp.array(slope_list(HEADS), F32) * LOG2E
+    small = jnp.stack([bias_q, bias_v, bias_out, ln1_gain, ln1_bias, bias_down, ln2_gain, ln2_bias])
+    small = lax.dynamic_update_slice(jnp.zeros((16, D), BF), small, (0, f * rows))
+    hbm = pl.BlockSpec(memory_space=pl.ANY)
+    smem = pl.BlockSpec(memory_space=pltpu.SMEM)
+    vmem = pl.BlockSpec(memory_space=pltpu.VMEM)
+    S = jax.ShapeDtypeStruct
+    T = pltpu.SemaphoreType.DMA
+    V = pltpu.VMEM
+    fw_outs = [
+        S((total, slots_here, D), BF), S((3, L, D), BF), S((L, D), BF), S((HEADS, 1, L), F32), S((L, D), F32),
+        S((total, slots_here, D), BF), S((3, Z, 2, 2, rows, D), BF), S((9, Z, 2, 2, rows, D), BF),
+        S((Z, 2, 2, 4, rows, D), BF), S((8, D), F32),
+    ]
+    fw = pl.pallas_call(
+        functools.partial(forward_kernel, fsdp, rows),
+        out_shape=fw_outs,
+        in_specs=[smem, smem] + [hbm] * 7,
+        out_specs=[hbm] * len(fw_outs),
+        scratch_shapes=[
+            V((12, Z, 2, 2, rows, D), BF), V((Z, 2, 2, 4, rows, D), BF),
+            V((total, slots_here, D), BF), V((total, slots_here, D), BF),
+            V((fsdp, 16, D), BF), V((16, D), F32), V((3, L, D), BF), V((L, L), F32), V((HEADS, 1, L), F32),
+            V((L, D), BF), V((L, D), F32), V((L, D), BF), V((L, D), F32), V((L, 128), F32),
+            V((L, FF), BF), V((L, FF), BF), V((L, FF), BF), V((L, D), F32), V((L, D), BF), V((D, L), BF),
+            *Gather.sems(Z), T((3,)), T((3,)), T((3,)), T((11,)), V((total, slots_here, D), BF), V((8, D), F32),
+        ],
+        compiler_params=pltpu.CompilerParams(collective_id=0, has_side_effects=True, vmem_limit_bytes=VMEM_LIMIT),
+        name="gather_and_forward",
+    )(length, slopes, dealt, grads, small, w_qkv, w_out, w_gate_up, w_down)
+    x, qkv, dob, lse, h1, out, wqkv, dwa, dwd, smallg = fw
+    bw_outs = [
+        S((rows, 3 * D), F32), S((rows, D), F32), S((rows, 2 * FF), F32), S((4 * rows, D), F32),
+        S((total, slots_here, D), BF), S((total, slots_here, D), BF), S((8, D), F32),
+    ]
+    gq, gw, gg, gd, output, dealt_grads, small_sum = pl.pallas_call(
+        functools.partial(backward_kernel, fsdp, rows),
+        out_shape=bw_outs,
+        in_specs=[smem, smem] + [hbm] * 10,
+        out_specs=[vmem] * 4 + [hbm] * 2 + [vmem],
+        scratch_shapes=[
+            V((total, slots_here, D), BF), V((3, L, D), BF), V((L, D), BF), V((HEADS, 1, L), F32), V((L, D), F32),
+            V((3, Z, 2, 2, rows, D), BF), V((L, L), F32), V((3, L, D), BF), V((3, Z, 2, 2, rows, D), BF),
+            V((total, slots_here, D), BF), V((8, D), F32), V((total, 8, D), F32),
+            *Scatter.buffers(Z, rows), *Scatter.sems(), T((3,)), T((3,)), T((3,)), T((7,)),
+        ],
+        compiler_params=pltpu.CompilerParams(collective_id=1, has_side_effects=True, vmem_limit_bytes=VMEM_LIMIT),
+        name="backward_and_scatter",
+    )(length, slopes, x, qkv, dob, lse, h1, out, wqkv, dwa, dwd, smallg)
+    inverse = jnp.argsort(order, axis=1)
+    input_grad = jnp.take_along_axis(
+        dealt_grads.reshape(tokens_in.shape), inverse[:, :, None, None], axis=1
+    )
+    mine = lax.dynamic_slice(small_sum, (0, f * rows), (8, rows))
+    return (
+        output.reshape(tokens_in.shape), input_grad, gq, mine[BQ], mine[BV], gw, mine[BO], mine[G1], mine[B1], gg, gd,
+        mine[BD], mine[G2], mine[B2],
+    )
+
+
 def solution(mesh):
+    fsdp = mesh.shape["fsdp"]
+    rows = D // fsdp
+    kernels = mesh.shape["ctx"] == M and fsdp == 16 and rows % 16 == 0
     return jax.shard_map(
-        per_device,
+        per_device if kernels else per_device_plain,
         mesh=mesh,
         in_specs=(
             P(None, None, ("ctx", "fsdp"), None),

time: 1460 us -> 325 us (0.22)
  waiting for transfers between devices: 948 us -> 0 us
  Pallas kernels: 0 us -> 299 us
  blocking collectives: 182 us -> 0 us
  matrix products: 154 us -> 0 us
  other arithmetic: 84.6 us -> 4.15 us
  local copies, waits for them, and re-layouts: 43 us -> 12 us
  starting transfers between devices: 21.5 us -> 0 us
    reduce_scatter x12 -> x0, waiting for transfers between devices: 884 us -> none  [the longest x2 393 us: reduce_grads(): lax.psum_scatter(grad_terms[7], 'fsdp', scatter_dimension=0, tiled=True)]
    pallas_call x0 -> x2, Pallas kernels: none -> 299 us  [the longest x1 167 us: per_device(): pl.pallas_call(functools.partial(forward_kernel, fsdp, rows), out_shape=f...]
    dot_general x36 -> x0, matrix products: 154 us -> none  [the longest x8 52.7 us: rows_product(): lax.dot_general(former, latter, (((0,), (0,)), ((), ())), preferred_eleme...]
    unnamed x2 -> x0, blocking collectives: 133 us -> none
    all_gather x4 -> x0, blocking collectives: 44 us -> none  [the longest x2 23.5 us: per_device(): lax.all_gather(key_rows, 'ctx', axis=0, tiled=True)]
    convert_element_type x22 -> x0, other arithmetic: 42.1 us -> none  [the longest x2 16.2 us: per_device(): hidden_low = hidden.astype(jnp.bfloat16)]
    all_gather x4 -> x0, waiting for transfers between devices: 39.8 us -> none  [the longest x1 28.2 us: fetch_weights(): lax.all_gather(shards[8], 'fsdp', axis=0, tiled=True)]
    all_to_all x4 -> x0, waiting for transfers between devices: 22 us -> none  [the longest x1 12.5 us: per_device(): lax.all_to_all(output_stack, 'fsdp', split_axis=2, concat_axis=1, tiled=T...]
  transfers between devices with their start and end apart: 21 -> 0, of which waited for: 13 -> 0; matrix products, arithmetic and copies ran while one was open for 14% -> 0% of each run, Pallas kernels for 0% -> 0%
where the time goes in v1:
time: 325 us; the launch traced here: 318 us
  Pallas kernels  299 us (92%)
  local copies, waits for them, and re-layouts  12 us (4%)
  other arithmetic  4.15 us (1%)
    pallas_call x1, Pallas kernels, per_device(): pl.pallas_call(functools.partial(forward_kernel, fsdp, rows), out_shape=f...  167 us
    pallas_call x1, Pallas kernels, per_device(): pl.pallas_call(functools.partial(backward_kernel, fsdp, rows), out_shape=...  132 us

profile of v1, /device:TPU:0, one launch (start us, length us, event | category | flops | bytes accessed | tf_op | source)
XLA Modules:
  0.0 318.2 jit_solution(463954318352819139)
XLA Ops:
  0.6 0.0 copy-start
  0.7 1.3 dynamic_slice.9
  3.9 1.3 dynamic_slice.10
  5.2 0.8 stack.35
  6.0 0.3 dynamic_update_slice.3.small_in
  6.4 0.0 copy-start.6
  6.4 0.7 bitcast_or_fusion.1
  7.1 0.1 reshape.86
  7.1 0.0 copy-done
  7.1 0.6 gather_fusion
  7.8 0.7 and_bitcast_fusion.1
  8.5 1.0 broadcast_select_fusion.1
  9.5 0.0 copy-done.6
  9.5 167.3 %gather_and_forward.1 = (bf16[32,16,768]{2,1,0:T(8,128)(2,1)}, bf16[3,512,768]{2,1,0:T(8,128)(2,1)}, bf16[512,768]{1,0:T(8,128)(2,1)}, f32[12,1,512]{2,1,0:T(1,1...) custom-call(s32[1]{0:T(128)} %bitcast.1.length, ...), custom_call_target="tpu_custom_call" | custom-call | tf_op jit(solution)/shard_map/gather_and_forward/pallas_call | solution.py:1109
  176.8 0.0 copy-start.7
  176.8 131.6 %backward_and_scatter.1 = (f32[48,2304]{1,0:T(8,128)}, f32[48,768]{1,0:T(8,128)}, f32[48,6144]{1,0:T(8,128)}, f32[192,768]{1,0:T(8,128)}, bf16[32,16,768]{2,1,0:...) custom-call(s32[1]{0:T(128)} %bitcast.1.length, f32[12]{0:T(128)} %constant.38.slopes, ...), custom_call_target="tpu_custom_call" | custom-call | tf_op jit(solution)/shard_map/backward_and_scatter/pallas_call | solution.py:1130
  308.4 0.0 copy-start.2
  308.4 0.0 copy-done.7
  308.4 0.1 copy.31
  308.5 0.7 sort.17
  309.2 0.1 copy.32
  309.3 0.1 reshape.91
  309.4 0.0 copy-start.4
  309.4 1.8 gather_fusion.1
  311.2 0.0 copy-start.5
  311.2 0.0 copy-start.1
  311.3 1.0 broadcast_select_fusion
  312.3 0.8 constant_dynamic-slice_fusion
  313.0 0.5 slice_bitcast_fusion
  313.6 0.0 copy-done.2
  313.6 0.0 copy-start.3
  313.6 0.9 copy.39
  314.5 0.0 copy-done.4
  314.5 0.8 copy.40
  315.2 0.0 copy-done.5
  315.2 0.7 copy.41
  315.9 0.0 copy-done.1
  315.9 1.0 copy.42
  316.9 0.0 copy-done.3
  316.9 0.8 copy.43
  (4 shorter events, 0.0 us)
Async XLA Ops:
  0.6 6.5 %copy-start = (bf16[2,16,16,768]{3,2,1,0:T(8,128)(2,1)S(1)}, bf16[2,16,16,768]{3,2,1,0:T(8,128)(2,1)}, u32[]{:S(2)}) copy-start(bf16[2,16,16,768]{3,2,1,0:T(8,128)(2,1)} %param.19) | copy-start | bytes 2359300
  6.4 3.1 copy-start.6
  176.8 131.6 %copy-start.7 = (s32[2,16]{1,0:T(2,128)S(1)}, s32[2,16]{1,0:T(2,128)}, u32[]{:S(2)}) copy-start(s32[2,16]{1,0:T(2,128)} %param.22) | copy-start | bytes 388
  308.4 5.2 %copy-start.2 = (bf16[32,16,768]{2,1,0:T(8,128)(2,1)S(1)}, bf16[32,16,768]{2,1,0:T(8,128)(2,1)}, u32[]{:S(2)}) copy-start(bf16[32,16,768]{2,1,0:T(8,128)(2,1)} %get-tuple-element.43) | copy-start | bytes 2359300
  309.4 5.1 %copy-start.4 = (f32[48,2304]{1,0:T(8,128)S(1)}, f32[48,2304]{1,0:T(8,128)}, u32[]{:S(2)}) copy-start(f32[48,2304]{1,0:T(8,128)} %get-tuple-element.75) | copy-start | bytes 1327108
  311.2 4.0 %copy-start.5 = (f32[48,768]{1,0:T(8,128)S(1)}, f32[48,768]{1,0:T(8,128)}, u32[]{:S(2)}) copy-start(f32[48,768]{1,0:T(8,128)} %get-tuple-element.78) | copy-start | bytes 442372
  311.2 4.7 %copy-start.1 = (f32[48,6144]{1,0:T(8,128)S(1)}, f32[48,6144]{1,0:T(8,128)}, u32[]{:S(2)}) copy-start(f32[48,6144]{1,0:T(8,128)} %get-tuple-element.82) | copy-start | bytes 3538948
  313.6 3.3 %copy-start.3 = (f32[192,768]{1,0:T(8,128)S(1)}, f32[192,768]{1,0:T(8,128)}, u32[]{:S(2)}) copy-start(f32[192,768]{1,0:T(8,128)} %get-tuple-element.83) | copy-start | bytes 1769476
